TPU v7x, 32 devices: a whole 2x2x4 slice. The times are simulated.
32 devices in a mesh: groups: 2 (over x), train: 16 (over z, y, core).
Axes of the slice: x: 2, y: 2, z: 4, core: 2. Of those that a mesh axis runs over, the one named last changes fastest.
Arguments:
- train_grads: bfloat16 [4, 20480, 4096], P(None, ('groups', 'train')), parts along dimension 1, may hold values from -300 to 300
- token_counts: int32 [20480], P(('groups', 'train')), parts along dimension 0, may hold values from 64 to 511
- queries: bfloat16 [4, 128, 4096], P(None, ('groups', 'train')), parts along dimension 1, may hold values from -6 to 6
- basis_out: float32 [4, 64, 64], replicated, may hold values from -0.75 to 0.75
- basis_in: float32 [4, 64, 64], replicated, may hold values from -0.75 to 0.75
- eig_out: float32 [4, 64], replicated, may hold values from 0.3 to 3
- eig_in: float32 [4, 64], replicated, may hold values from 0.3 to 3
Outputs:
- influence: float32 [20480, 64], P(('groups', 'train')), parts along dimension 0
There are 2 independent parts, one for each index of `groups`. A program takes and returns all parts, laid end to end along the dimension named above; an argument that names none is the same for every part. Nothing has to cross between parts.
All inputs are finite; a program needn't handle non-finite values.
Results may differ from a plain program's by a relative error of at most 0.003.
Values may be sent and summed in bfloat16 or wider, within the bound.
A program may use at most 128 MiB of HBM per device.

v0:
```python
import jax
import jax.numpy as jnp
from jax import lax
from jax.sharding import PartitionSpec as P


def precondition(raw, basis_out, basis_in, eig_out, eig_in):
    layers, count, proj = raw.shape
    width = basis_out.shape[1]
    hi = lax.Precision.HIGHEST
    field = raw.astype(jnp.float32).reshape(layers, count, width, width)
    rotated = jnp.einsum("lnjk,lkm->lnjm", field, basis_in, precision=hi)
    rotated = jnp.einsum("lji,lnjm->lnim", basis_out, rotated, precision=hi)
    spectrum = eig_out[:, :, None] * eig_in[:, None, :] + 0.01
    scaled = rotated / spectrum[:, None]
    back = jnp.einsum("lnjk,lmk->lnjm", scaled, basis_in, precision=hi)
    back = jnp.einsum("lij,lnjm->lnim", basis_out, back, precision=hi)
    return back.reshape(layers, count, proj).astype(jnp.bfloat16)


def per_device(train_grads, token_counts, queries, basis_out, basis_in, eig_out, eig_in):
    mine = precondition(queries, basis_out, basis_in, eig_out, eig_in)
    everyone = lax.all_gather(mine, "train", axis=1, tiled=True)
    total = jnp.zeros((train_grads.shape[1], everyone.shape[1]), jnp.float32)
    for layer in range(train_grads.shape[0]):
        total = total + lax.dot_general(
            train_grads[layer], everyone[layer], (((1,), (1,)), ((), ())),
            preferred_element_type=jnp.float32,
        )
    scores = total / token_counts.astype(jnp.float32)[:, None]
    summed = lax.psum(jnp.sum(scores, axis=0), "train")
    column_mean = summed / (scores.shape[0] * lax.axis_size("train"))
    return scores - column_mean[None, :]


def solution(mesh):
    rows = P(None, ("groups", "train"), None)
    in_specs = (rows, P(("groups", "train")), rows, P(), P(), P(), P())
    return jax.shard_map(
        per_device, mesh=mesh, in_specs=in_specs,
        out_specs=P(("groups", "train"), None), check_vma=False,
    )
```

profile of v0, /device:TPU:0, one launch (start us, length us, event | category | flops | bytes accessed | tf_op | source)
XLA Modules:
  0.0 118.6 jit_solution(7223606267057350242)
XLA Ops:
  6.5 0.0 copy-start
  6.5 0.0 copy-start.1
  6.5 0.0 all-gather.2.cloned.1.call-start
  6.5 1.2 %reshape.11 = bf16[4,4,64,64]{3,2,1,0:T(8,128)(2,1)S(1)} reshape(bf16[4,4,4096]{2,1,0:T(4,128)(2,1)} %param.9) | data formatting | bytes 262144 | tf_op jit(solution)/shard_map/reshape | solution.py:11
  7.7 0.0 copy-done
  7.7 0.9 fusion.30
  8.6 0.8 multiply_add_fusion
  9.4 1.5 %fusion.12 = f32[4,4,64,64]{2,3,1,0:T(8,128)S(1)} fusion(f32[4,4,64,64]{2,3,1,0:T(8,128)S(1)} %fusion.30, f32[4,64,64]{1,2,0:T(8,128)S(1)} %multiply_add_fusion, f32[4,64,64]{2,1,0:T(8,128)} %param.10), kind=kOutput, calls=%fused_computation.13 | convolution fusion | flops 50397184 | bytes 655360 | tf_op jit(solution)/shard_map/lji,lnjm->lnim/dot_general | solution.py:13
  10.9 0.6 fusion.28
  11.5 1.5 %fusion.13 = bf16[4,4,64,64]{2,3,1,0:T(8,128)(2,1)S(1)} fusion(f32[4,4,64,64]{2,3,1,0:T(8,128)S(1)} %fusion.28, f32[4,64,64]{2,1,0:T(8,128)} %param.10), kind=kOutput, calls=%fused_computation.15 | convolution fusion | flops 50397184 | bytes 458752 | tf_op jit(solution)/shard_map/lij,lnjm->lnim/dot_general | solution.py:17
  13.1 0.2 copy.28
  13.2 0.9 reshape.14
  14.1 0.0 all-gather.2.cloned.1.call-update
  14.2 0.0 copy-done.1
  14.2 44.2 %all-gather.2.cloned.1.call-done = bf16[4,64,4096]{2,0,1:T(4,128)(2,1)} async-done(((bf16[4,4,4096]{2,0,1:T(4,128)(2,1)}), bf16[4,64,4096]{2,0,1:T(4,128)(2,1)}) %all-gather.2.cloned.1.call-update) | async-done | bytes 2097168 | tf_op jit(solution)/shard_map/all_gather | solution.py:23
  58.4 0.0 copy-start.2
  58.4 8.8 %fusion.32 = (bf16[1,64,4096]{2,0,1:T(2,128)(2,1)S(1)}, bf16[1,64,4096]{2,0,1:T(2,128)(2,1)S(1)}, bf16[1,64,4096]{2,0,1:T(2,128)(2,1)S(1)}, bf16[1,64,4096]{2,0,1:T(2,128)(2,1)S(1)}) fusion(bf16[4,64,4096]{2,0,1:T(4,128)(2,1)} %all-gather.2.cloned.1.call-done), kind=kLoop, calls=%fused_computation.33 | loop fusion | bytes 4194304 | tf_op jit(solution)/shard_map/slice | solution.py:27
  67.2 4.3 %fusion = f32[64,640]{1,0:T(8,128)S(1)} fusion(bf16[4,640,4096]{2,1,0:T(8,128)(2,1)} %param.7, bf16[1,64,4096]{2,0,1:T(2,128)(2,1)S(1)} %get-tuple-element.8), kind=kOutput, calls=%fused_computation | convolution fusion | flops 335544320 | bytes 5931008 | tf_op jit(solution)/shard_map/dot_general | solution.py:26
  71.5 4.3 %fusion.2 = f32[64,640]{1,0:T(8,128)S(1)} fusion(bf16[4,640,4096]{2,1,0:T(8,128)(2,1)} %param.7, bf16[1,64,4096]{2,0,1:T(2,128)(2,1)S(1)} %get-tuple-element.6), kind=kOutput, calls=%fused_computation.2 | convolution fusion | flops 335544320 | bytes 5931008 | tf_op jit(solution)/shard_map/dot_general | solution.py:26
  75.8 0.0 copy-done.2
  75.8 1.8 %fusion.4 = f32[64,640]{1,0:T(8,128)S(1)} fusion(bf16[4,640,4096]{2,1,0:T(8,128)(2,1)S(1)} %copy-done.2, bf16[1,64,4096]{2,0,1:T(2,128)(2,1)S(1)} %get-tuple-element.7), kind=kOutput, calls=%fused_computation.4 | convolution fusion | flops 335544320 | bytes 6455296 | tf_op jit(solution)/shard_map/dot_general | solution.py:26
  77.6 1.9 %fusion.33 = (f32[64]{0:T(128)S(1)}, f32[64,640]{1,0:T(8,128)S(1)}) fusion(f32[640]{0:T(1024)S(1)} %convert_element_type.16, f32[64,640]{1,0:T(8,128)S(1)} %fusion, f32[64,640]{1,0:T(8,128)S(1)} %fusion.2, f32[64,640]{1,0:T(8,128)S(1)} %fusion.4, bf16[4,640,4096]{2,1,0:T(8,128)(2,1)S(1)} %copy-done.2, bf16[1,64,4096]{2,0,1:T(2,128)(2,1)S(1)} %get-tuple-element.5), kind=kOutput, calls=%fused_computation.34 | convolution fusion | flops 335749056 | bytes 6951168 | tf_op jit(solution)/shard_map/dot_general | solution.py:26
  79.6 31.4 %psum.7 = f32[64]{0:T(128)S(1)} all-reduce(f32[64]{0:T(128)S(1)} %get-tuple-element.9), channel_id=1, replica_groups=mesh['groups'=2,'train'=16] {'train'}, use_global_device_ids=true, to_apply=%region_1.0 | all-reduce | flops 64 | bytes 512 | tf_op jit(solution)/shard_map/psum | solution.py:31
  111.0 0.7 subtract_bitcast_fusion
  (2 shorter events, 0.0 us)
Async XLA Ops:
  6.5 1.2 %copy-start = (f32[4,64,64]{2,1,0:T(8,128)S(1)}, f32[4,64,64]{2,1,0:T(8,128)}, u32[]{:S(2)}) copy-start(f32[4,64,64]{2,1,0:T(8,128)} %param.11) | copy-start | bytes 196612
  6.5 7.6 %copy-start.1 = (s32[640]{0:T(1024)S(1)}, s32[640]{0:T(1024)}, u32[]{:S(2)}) copy-start(s32[640]{0:T(1024)} %param.8) | copy-start | bytes 7684
  6.5 51.9 %all-gather.2.cloned.1.call-start = ((), (), s32[]{:S(2)}) async-start(), calls=%async_computation | async-start | bytes 2228224 | tf_op jit(solution)/shard_map/all_gather | solution.py:23
  58.4 17.4 %copy-start.2 = (bf16[4,640,4096]{2,1,0:T(8,128)(2,1)S(1)}, bf16[4,640,4096]{2,1,0:T(8,128)(2,1)}, u32[]{:S(2)}) copy-start(bf16[4,640,4096]{2,1,0:T(8,128)(2,1)} %param.7) | copy-start | bytes 62914564
Sparse Core Ops, SparseCore 0:
  14.3 44.0 all-gather.1
where the time goes:
time: 119 us
  waiting for transfers between devices  44.2 us (37%)
  blocking collectives  31.4 us (26%)
  matrix products  16.8 us (14%)
  between operations  13.5 us (11%)
  local copies, waits for them, and re-layouts  11 us (9%)
  other arithmetic  1.56 us (1%)
    all_gather x1, waiting for transfers between devices, per_device(): everyone = lax.all_gather(mine, 'train', axis=1, tiled=True)  44.2 us
    psum x1, blocking collectives, per_device(): summed = lax.psum(jnp.sum(scores, axis=0), 'train')  31.4 us
    dot_general x4, matrix products, per_device(): lax.dot_general(train_grads[layer], everyone[layer], (((1,), (1,)), ((),...  12.4 us
    slice x1, local copies, waits for them, and re-layouts, per_device(): everyone[layer]  8.76 us
  transfers between devices with their start and end apart: 1, of which 1 were waited for; matrix products, arithmetic and copies ran while one was open for 0% of the time, Pallas kernels for 0%

commit v1 on v0

v1 whole, which is shorter than its diff:
```python
import functools

import jax
import jax.numpy as jnp
from jax import lax
from jax.experimental import pallas as pl
from jax.experimental.pallas import tpu as pltpu
from jax.sharding import PartitionSpec as P

CHUNKS = 4
HIGHEST = lax.Precision.HIGHEST


def precondition(raw, basis_out, basis_in, eig_out, eig_in):
    layers, count, proj = raw.shape
    width = basis_out.shape[1]
    field = raw.astype(jnp.float32).reshape(layers, count, width, width)
    rotated = jnp.einsum("lnjk,lkm->lnjm", field, basis_in, precision=HIGHEST)
    rotated = jnp.einsum("lji,lnjm->lnim", basis_out, rotated, precision=HIGHEST)
    spectrum = eig_out[:, :, None] * eig_in[:, None, :] + 0.01
    scaled = rotated / spectrum[:, None]
    back = jnp.einsum("lnjk,lmk->lnjm", scaled, basis_in, precision=HIGHEST)
    back = jnp.einsum("lij,lnjm->lnim", basis_out, back, precision=HIGHEST)
    return back.reshape(layers, count, proj).astype(jnp.bfloat16)


def plain(train_grads, token_counts, queries, basis_out, basis_in, eig_out, eig_in):
    mine = precondition(queries, basis_out, basis_in, eig_out, eig_in)
    everyone = lax.all_gather(mine, "train", axis=1, tiled=True)
    total = jnp.zeros((train_grads.shape[1], everyone.shape[1]), jnp.float32)
    for layer in range(train_grads.shape[0]):
        total = total + lax.dot_general(
            train_grads[layer], everyone[layer], (((1,), (1,)), ((), ())),
            preferred_element_type=jnp.float32,
        )
    scores = total / token_counts.astype(jnp.float32)[:, None]
    summed = lax.psum(jnp.sum(scores, axis=0), "train")
    column_mean = summed / (scores.shape[0] * lax.axis_size("train"))
    return scores - column_mean[None, :]


def kernel(
    devices, layers, mine_ref, counts_ref, train_ref, out_ref,
    held, rows_of, sums, load_sem, send_sem, recv_sem, sum_send, sum_recv,
):
    me = lax.axis_index("train")
    depth = devices // 4
    z, y, core = me // 4, (me // 2) % 2, me % 2
    local, proj = mine_ref.shape
    wide = proj // CHUNKS
    count = local // layers

    def slot(zz, yy, cc):
        return (zz * 2 + yy) * 2 + cc

    barrier = pltpu.get_barrier_semaphore()
    for step in range(1, devices):
        pl.semaphore_signal(
            barrier, inc=1, device_id={"train": (me + step) % devices},
            device_id_type=pl.DeviceIdType.MESH,
        )

    loads = []
    for chunk in range(CHUNKS):
        cols = pl.ds(chunk * wide, wide)
        loads.append([])
        for layer in range(layers):
            copy = pltpu.make_async_copy(
                train_ref.at[layer, :, cols],
                rows_of.at[chunk, :, pl.ds(layer * wide, wide)],
                load_sem.at[chunk, layer],
            )
            copy.start()
            loads[-1].append(copy)

    held[me] = mine_ref[...]
    pl.semaphore_wait(barrier, devices - 1)

    sent = []

    def send(chunk, which, number, target):
        part = held.at[which, :, pl.ds(chunk * wide, wide)]
        copy = pltpu.make_async_remote_copy(
            src_ref=part, dst_ref=part,
            send_sem=send_sem.at[chunk, number], recv_sem=recv_sem.at[chunk, which],
            device_id={"train": target}, device_id_type=pl.DeviceIdType.MESH,
        )
        copy.start()
        sent.append(copy)

    def arrive(chunk, which):
        part = held.at[which, :, pl.ds(chunk * wide, wide)]
        pltpu.make_async_remote_copy(
            src_ref=part, dst_ref=part,
            send_sem=send_sem.at[chunk, 0], recv_sem=recv_sem.at[chunk, which],
            device_id={"train": me}, device_id_type=pl.DeviceIdType.MESH,
        ).wait_recv()

    across = slot(z, 1 - y, core)
    sibling = slot(z, y, 1 - core)
    for chunk in range(CHUNKS):
        for step in range(1, depth):
            send(chunk, me, step - 1, slot((z + step) % depth, y, core))
        send(chunk, me, depth - 1, across)
        send(chunk, me, 2 * depth - 1, sibling)

    def forward(chunk):
        for step in range(1, depth):
            which = slot((z + step) % depth, y, core)
            arrive(chunk, which)
            send(chunk, which, depth - 1 + step, across)
            send(chunk, which, 2 * depth - 1 + step, sibling)
        for step in range(depth):
            which = slot((z + step) % depth, 1 - y, core)
            arrive(chunk, which)
            send(chunk, which, 3 * depth - 1 + step, sibling)

    total_rows = devices * local
    layer_of = (lax.broadcasted_iota(jnp.int32, (total_rows, 128), 0) // count) % layers
    masks = [
        jnp.where(layer_of == layer, 1.0, 0.0).astype(jnp.bfloat16) for layer in range(layers)
    ]

    def contract(chunk):
        for yy in range(2):
            for step in range(depth):
                arrive(chunk, slot((z + step) % depth, (y + yy) % 2, 1 - core))
        for copy in loads[chunk]:
            copy.wait()
        block = held[:, :, pl.ds(chunk * wide, wide)].reshape(total_rows, wide)
        spread = [jnp.concatenate([mask] * (wide // 128), axis=1) for mask in masks]
        right = jnp.concatenate([block * m for m in spread], axis=1)
        return lax.dot_general(
            rows_of[chunk], right, (((1,), (1,)), ((), ())),
            preferred_element_type=jnp.float32,
        )

    forward(0)
    total = None
    for chunk in range(CHUNKS):
        if chunk + 1 < CHUNKS:
            forward(chunk + 1)
        part = contract(chunk)
        total = part if total is None else total + part

    scores = total / counts_ref[...].astype(jnp.float32)
    sums[me] = jnp.sum(scores, axis=0, keepdims=True)
    told = []
    for step in range(1, devices):
        copy = pltpu.make_async_remote_copy(
            src_ref=sums.at[me], dst_ref=sums.at[me],
            send_sem=sum_send.at[step], recv_sem=sum_recv.at[me],
            device_id={"train": (me + step) % devices}, device_id_type=pl.DeviceIdType.MESH,
        )
        copy.start()
        told.append(copy)

    queries = devices * count
    source = lax.broadcasted_iota(jnp.int32, (total_rows, queries), 0)
    column = lax.broadcasted_iota(jnp.int32, (total_rows, queries), 1)
    pick = (source // local) * count + source % count == column
    pick = jnp.where(pick, 1.0, 0.0)
    scores = jnp.dot(scores, pick, precision=HIGHEST, preferred_element_type=jnp.float32)
    for step in range(1, devices):
        which = (me + step) % devices
        pltpu.make_async_remote_copy(
            src_ref=sums.at[which], dst_ref=sums.at[which],
            send_sem=sum_send.at[0], recv_sem=sum_recv.at[which],
            device_id={"train": me}, device_id_type=pl.DeviceIdType.MESH,
        ).wait_recv()
    summed = sums[0]
    for which in range(1, devices):
        summed = summed + sums[which]
    mean = summed * (1.0 / (devices * scores.shape[0]))
    mean = jnp.broadcast_to(mean, (8, total_rows))
    mean = jnp.dot(mean, pick, precision=HIGHEST, preferred_element_type=jnp.float32)
    out_ref[...] = scores - mean[0:1]
    for copy in sent + told:
        copy.wait_send()


def fused(train_grads, token_counts, queries, basis_out, basis_in, eig_out, eig_in):
    layers, rows, proj = train_grads.shape
    devices = lax.axis_size("train")
    count = queries.shape[1]
    mine = precondition(queries, basis_out, basis_in, eig_out, eig_in)
    mine = mine.reshape(layers * count, proj)
    local = layers * count
    wide = proj // CHUNKS
    vmem = pl.BlockSpec(memory_space=pltpu.VMEM)
    return pl.pallas_call(
        functools.partial(kernel, devices, layers),
        out_shape=jax.ShapeDtypeStruct((rows, devices * count), jnp.float32),
        in_specs=[vmem, vmem, pl.BlockSpec(memory_space=pl.ANY)],
        out_specs=vmem,
        scratch_shapes=[
            pltpu.VMEM((devices, local, proj), jnp.bfloat16),
            pltpu.VMEM((CHUNKS, rows, layers * wide), jnp.bfloat16),
            pltpu.VMEM((devices, 1, devices * local), jnp.float32),
            pltpu.SemaphoreType.DMA((CHUNKS, layers)),
            pltpu.SemaphoreType.DMA((CHUNKS, devices)),
            pltpu.SemaphoreType.DMA((CHUNKS, devices)),
            pltpu.SemaphoreType.DMA((devices,)),
            pltpu.SemaphoreType.DMA((devices,)),
        ],
        compiler_params=pltpu.CompilerParams(
            collective_id=0, has_side_effects=True, vmem_limit_bytes=56 * 2**20
        ),
        cost_estimate=pl.CostEstimate(
            flops=2 * rows * layers * proj * devices * count,
            bytes_accessed=layers * rows * proj * 2, transcendentals=0,
        ),
    )(mine, token_counts.reshape(rows, 1), train_grads)


def solution(mesh):
    devices = mesh.shape["train"]

    def per_device(train_grads, token_counts, queries, *factors):
        layers, rows, proj = train_grads.shape
        local = layers * queries.shape[1]
        fits = devices % 4 == 0 and local % 16 == 0 and proj % (128 * CHUNKS) == 0
        fits = fits and devices * local <= 512 and rows % 16 == 0
        fits = fits and layers * rows * proj <= 12 * 2**20
        body = fused if fits else plain
        return body(train_grads, token_counts, queries, *factors)

    rows = P(None, ("groups", "train"), None)
    in_specs = (rows, P(("groups", "train")), rows, P(), P(), P(), P())
    return jax.shard_map(
        per_device, mesh=mesh, in_specs=in_specs,
        out_specs=P(("groups", "train"), None), check_vma=False,
    )
```

time: 119 us -> 56.7 us (0.48)
  Pallas kernels: 0 us -> 45.6 us
  waiting for transfers between devices: 44.2 us -> 0 us
  blocking collectives: 31.4 us -> 0 us
  between operations: 13.5 us -> 0.07 us
  matrix products: 16.8 us -> 4.35 us
  local copies, waits for them, and re-layouts: 11 us -> 5.61 us
    pallas_call x0 -> x1, Pallas kernels: none -> 45.6 us  [fused(): pl.pallas_call(functools.partial(kernel, devices, layers), out_shape=jax....]
    all_gather x1 -> x0, waiting for transfers between devices: 44.2 us -> none  [per_device(): everyone = lax.all_gather(mine, 'train', axis=1, tiled=True)]
    psum x1 -> x0, blocking collectives: 31.4 us -> none  [per_device(): summed = lax.psum(jnp.sum(scores, axis=0), 'train')]
    dot_general x8 -> x4, matrix products: 16.8 us -> 4.35 us  [the longest x1 1.9 us: precondition(): jnp.einsum('lji,lnjm->lnim', basis_out, rotated, precision=HIGHEST)]
    slice x1 -> x0, local copies, waits for them, and re-layouts: 8.76 us -> none  [per_device(): everyone[layer]]
    pallas_call x0 -> x1, local copies, waits for them, and re-layouts: none -> 1.79 us  [fused(): pl.pallas_call(functools.partial(kernel, devices, layers), out_shape=jax....]
    reshape x0 -> x1, local copies, waits for them, and re-layouts: none -> 1.55 us  [fused(): token_counts.reshape(rows, 1)]
  transfers between devices with their start and end apart: 1 -> 0, of which waited for: 1 -> 0; matrix products, arithmetic and copies ran while one was open for 0% -> 0% of each run, Pallas kernels for 0% -> 0%
where the time goes in v1:
time: 56.7 us; the launch traced here: 56.4 us
  Pallas kernels  45.6 us (80%)
  local copies, waits for them, and re-layouts  5.61 us (10%)
  matrix products  4.35 us (8%)
  other arithmetic  0.83 us (1%)
    pallas_call x1, Pallas kernels, fused(): pl.pallas_call(functools.partial(kernel, devices, layers), out_shape=jax....  45.6 us
    dot_general x1, matrix products, precondition(): jnp.einsum('lji,lnjm->lnim', basis_out, rotated, precision=HIGHEST)  1.9 us
    pallas_call x1, local copies, waits for them, and re-layouts, fused(): pl.pallas_call(functools.partial(kernel, devices, layers), out_shape=jax....  1.79 us
    reshape x1, local copies, waits for them, and re-layouts, fused(): token_counts.reshape(rows, 1)  1.55 us
    dot_general x1, matrix products, precondition(): back = jnp.einsum('lij,lnjm->lnim', basis_out, back, precision=HIGHEST)  1.5 us
    reshape x1, local copies, waits for them, and re-layouts, precondition(): field = raw.astype(jnp.float32).reshape(layers, count, width, width)  1.16 us

profile of v1, /device:TPU:0, one launch (start us, length us, event | category | flops | bytes accessed | tf_op | source)
XLA Modules:
  0.0 56.4 jit_solution(10339037766533532640)
XLA Ops:
  0.0 0.0 copy-start
  0.0 0.8 %multiply_add_fusion = f32[4,64,64]{1,2,0:T(8,128)S(1)} fusion(f32[4,64]{1,0:T(4,128)} %param.13, f32[4,64]{1,0:T(4,128)} %param.12), kind=kLoop, calls=%fused_computation.10 | loop fusion | flops 32768 | bytes 67584 | tf_op jit(solution)/shard_map/add | solution.py:20
  0.8 1.2 %reshape.14 = bf16[4,4,64,64]{3,2,1,0:T(8,128)(2,1)S(1)} reshape(bf16[4,4,4096]{2,1,0:T(4,128)(2,1)} %param.9) | data formatting | bytes 262144 | tf_op jit(solution)/shard_map/reshape | solution.py:17
  2.0 0.0 copy-done
  2.0 0.4 fusion.6
  2.4 1.9 %fusion = f32[4,4,64,64]{2,3,1,0:T(8,128)S(1)} fusion(f32[4,4,64,64]{3,2,1,0:T(8,128)S(1)} %fusion.6, f32[4,64,64]{1,2,0:T(8,128)S(1)} %multiply_add_fusion, f32[4,64,64]{2,1,0:T(8,128)} %param.10), kind=kOutput, calls=%fused_computation.1 | convolution fusion | flops 50397184 | bytes 655360 | tf_op jit(solution)/shard_map/lji,lnjm->lnim/dot_general | solution.py:19
  4.3 0.6 %fusion.4 = f32[4,4,64,64]{2,3,1,0:T(8,128)S(1)} fusion(f32[4,4,64,64]{2,3,1,0:T(8,128)S(1)} %fusion, f32[4,64,64]{2,1,0:T(8,128)S(1)} %copy-done), kind=kOutput, calls=%fused_computation.6 | convolution fusion | flops 50331648 | bytes 589824 | tf_op jit(solution)/shard_map/lnjk,lmk->lnjm/dot_general | solution.py:22
  4.9 1.5 %fusion.1 = bf16[4,4,64,64]{2,3,1,0:T(8,128)(2,1)S(1)} fusion(f32[4,4,64,64]{2,3,1,0:T(8,128)S(1)} %fusion.4, f32[4,64,64]{2,1,0:T(8,128)} %param.10), kind=kOutput, calls=%fused_computation.3 | convolution fusion | flops 50397184 | bytes 458752 | tf_op jit(solution)/shard_map/lij,lnjm->lnim/dot_general | solution.py:23
  6.4 0.2 copy.10
  6.6 0.9 %convert_element_type.13.mine_ref = bf16[16,4096]{1,0:T(8,128)(2,1)} reshape(bf16[4,4,64,64]{3,2,1,0:T(8,128)(2,1)S(1)} %copy.10) | data formatting | bytes 262144 | tf_op jit(solution)/shard_map/convert_element_type | solution.py:24
  7.5 1.5 %reshape.18.counts_ref = s32[640,1]{1,0:T(8,128)} reshape(s32[640]{0:T(1024)} %param.8) | data formatting | bytes 5120 | tf_op jit(solution)/shard_map/reshape | solution.py:213
  9.1 45.6 %shard_map.73 = f32[640,64]{1,0:T(8,128)} custom-call(bf16[16,4096]{1,0:T(8,128)(2,1)} %convert_element_type.13.mine_ref, s32[640,1]{1,0:T(8,128)} %reshape.18.counts_ref, bf16[4,640,4096]{2,1,0:T(8,128)(2,1)} %train_ref.1), custom_call_target="tpu_custom_call" | custom-call | flops 1342177280 | bytes 20971520 | tf_op jit(solution)/shard_map/pallas_call | solution.py:191
  54.6 1.8 %copy.12 = f32[640,64]{0,1:T(8,128)} copy(f32[640,64]{1,0:T(8,128)} %shard_map.73) | data formatting | bytes 327680 | tf_op jit(solution)/shard_map/pallas_call | solution.py:191
Async XLA Ops:
  0.0 2.0 %copy-start = (f32[4,64,64]{2,1,0:T(8,128)S(1)}, f32[4,64,64]{2,1,0:T(8,128)}, u32[]{:S(2)}) copy-start(f32[4,64,64]{2,1,0:T(8,128)} %param.11) | copy-start | bytes 196612

commit v2 on v1

--- a/solution.py
+++ b/solution.py
@@ -7,7 +7,7 @@
 from jax.experimental.pallas import tpu as pltpu
 from jax.sharding import PartitionSpec as P
 
-CHUNKS = 4
+CHUNKS = 2
 HIGHEST = lax.Precision.HIGHEST
 
 
@@ -39,16 +39,77 @@
     return scores - column_mean[None, :]
 
 
+def column_of(row):
+    parts = []
+    for start in range(0, row.shape[1], 128):
+        piece = row[:, start : start + 128]
+        size = piece.shape[1]
+        down = lax.broadcasted_iota(jnp.int32, (size, size), 0)
+        along = lax.broadcasted_iota(jnp.int32, (size, size), 1)
+        spread = jnp.where(down == along, jnp.broadcast_to(piece, (size, size)), 0.0)
+        parts.append(jnp.sum(spread, axis=1, keepdims=True))
+    return parts[0] if len(parts) == 1 else jnp.concatenate(parts, axis=0)
+
+
+def dot(a, b, over_a=1, over_b=0):
+    return lax.dot_general(
+        a, b, (((over_a,), (over_b,)), ((), ())),
+        precision=HIGHEST, preferred_element_type=jnp.float32,
+    )
+
+
+def condition_into(
+    mine, field, raw_ref, basis_out_ref, basis_in_ref, eig_out_ref, eig_in_ref
+):
+    layers, count, proj = raw_ref.shape
+    width = basis_out_ref.shape[1]
+    pairs, lanes = width // 2, 2 * width
+    for layer in range(layers):
+        raw = raw_ref[layer].astype(jnp.float32)
+        for k in range(pairs):
+            field[layer * count : (layer + 1) * count, k, :] = raw[:, k * lanes : (k + 1) * lanes]
+    new = lax.broadcasted_iota(jnp.int32, (width, width), 0)
+    old = lax.broadcasted_iota(jnp.int32, (width, width), 1)
+    order = jnp.where(2 * (new % pairs) + new // pairs == old, 1.0, 0.0)
+    half = lax.broadcasted_iota(jnp.int32, (lanes, lanes), 0) // width
+    other = lax.broadcasted_iota(jnp.int32, (lanes, lanes), 1) // width
+    for layer in range(layers):
+        block = field[layer * count : (layer + 1) * count].reshape(count * pairs, lanes)
+        basis = basis_in_ref[layer]
+        twice = jnp.concatenate([basis, basis], axis=1)
+        twice = jnp.where(half == other, jnp.concatenate([twice, twice], axis=0), 0.0)
+        left = dot(order, basis_out_ref[layer])
+        turned = dot(block, twice)
+        rows = [turned[q * pairs : (q + 1) * pairs] for q in range(count)]
+        even = jnp.concatenate([r[:, :width] for r in rows], axis=1)
+        odd = jnp.concatenate([r[:, width:] for r in rows], axis=1)
+        rotated = dot(left, jnp.concatenate([even, odd], axis=0), 0, 0)
+        wide = jnp.concatenate([eig_in_ref[layer : layer + 1, :]] * count, axis=1)
+        scaled = rotated / (column_of(eig_out_ref[layer : layer + 1, :]) * wide + 0.01)
+        back = dot(left, scaled)
+        rows = [
+            jnp.concatenate(
+                [back[:pairs, q * width : (q + 1) * width], back[pairs:, q * width : (q + 1) * width]],
+                axis=1,
+            )
+            for q in range(count)
+        ]
+        done = dot(jnp.concatenate(rows, axis=0), twice, 1, 1)
+        field[layer * count : (layer + 1) * count] = done.reshape(count, pairs, lanes)
+    for k in range(pairs):
+        mine[:, k * lanes : (k + 1) * lanes] = field[:, k, :].astype(jnp.bfloat16)
+
+
 def kernel(
-    devices, layers, mine_ref, counts_ref, train_ref, out_ref,
-    held, rows_of, sums, load_sem, send_sem, recv_sem, sum_send, sum_recv,
+    devices, layers, raw_ref, counts_ref, basis_out_ref, basis_in_ref, eig_out_ref, eig_in_ref,
+    train_ref, out_ref, held, rows_of, sums, field, load_sem, send_sem, recv_sem, sum_send, sum_recv,
 ):
     me = lax.axis_index("train")
     depth = devices // 4
     z, y, core = me // 4, (me // 2) % 2, me % 2
-    local, proj = mine_ref.shape
+    count, proj = raw_ref.shape[1:]
+    local = layers * count
     wide = proj // CHUNKS
-    count = local // layers
 
     def slot(zz, yy, cc):
         return (zz * 2 + yy) * 2 + cc
@@ -73,7 +134,10 @@
             copy.start()
             loads[-1].append(copy)
 
-    held[me] = mine_ref[...]
+    condition_into(
+        held.at[me], field, raw_ref, basis_out_ref, basis_in_ref, eig_out_ref, eig_in_ref
+    )
+    inverse = column_of(1.0 / counts_ref[...].astype(jnp.float32))
     pl.semaphore_wait(barrier, devices - 1)
 
     sent = []
@@ -143,7 +207,7 @@
         part = contract(chunk)
         total = part if total is None else total + part
 
-    scores = total / counts_ref[...].astype(jnp.float32)
+    scores = total * inverse
     sums[me] = jnp.sum(scores, axis=0, keepdims=True)
     told = []
     for step in range(1, devices):
@@ -156,11 +220,13 @@
         told.append(copy)
 
     queries = devices * count
-    source = lax.broadcasted_iota(jnp.int32, (total_rows, queries), 0)
-    column = lax.broadcasted_iota(jnp.int32, (total_rows, queries), 1)
+    source = lax.broadcasted_iota(jnp.int32, (queries, total_rows), 1)
+    column = lax.broadcasted_iota(jnp.int32, (queries, total_rows), 0)
     pick = (source // local) * count + source % count == column
-    pick = jnp.where(pick, 1.0, 0.0)
-    scores = jnp.dot(scores, pick, precision=HIGHEST, preferred_element_type=jnp.float32)
+    flat = lax.dot_general(
+        jnp.where(pick, 1.0, 0.0), scores, (((1,), (1,)), ((), ())),
+        precision=HIGHEST, preferred_element_type=jnp.float32,
+    )
     for step in range(1, devices):
         which = (me + step) % devices
         pltpu.make_async_remote_copy(
@@ -172,9 +238,9 @@
     for which in range(1, devices):
         summed = summed + sums[which]
     mean = summed * (1.0 / (devices * scores.shape[0]))
-    mean = jnp.broadcast_to(mean, (8, total_rows))
-    mean = jnp.dot(mean, pick, precision=HIGHEST, preferred_element_type=jnp.float32)
-    out_ref[...] = scores - mean[0:1]
+    mean = jnp.broadcast_to(mean, (queries, total_rows))
+    mean = jnp.sum(jnp.where(pick, mean, 0.0), axis=1, keepdims=True)
+    out_ref[...] = flat - mean
     for copy in sent + told:
         copy.wait_send()
 
@@ -183,20 +249,19 @@
     layers, rows, proj = train_grads.shape
     devices = lax.axis_size("train")
     count = queries.shape[1]
-    mine = precondition(queries, basis_out, basis_in, eig_out, eig_in)
-    mine = mine.reshape(layers * count, proj)
     local = layers * count
     wide = proj // CHUNKS
     vmem = pl.BlockSpec(memory_space=pltpu.VMEM)
-    return pl.pallas_call(
+    flat = pl.pallas_call(
         functools.partial(kernel, devices, layers),
-        out_shape=jax.ShapeDtypeStruct((rows, devices * count), jnp.float32),
-        in_specs=[vmem, vmem, pl.BlockSpec(memory_space=pl.ANY)],
+        out_shape=jax.ShapeDtypeStruct((devices * count, rows), jnp.float32),
+        in_specs=[vmem] * 6 + [pl.BlockSpec(memory_space=pl.ANY)],
         out_specs=vmem,
         scratch_shapes=[
             pltpu.VMEM((devices, local, proj), jnp.bfloat16),
             pltpu.VMEM((CHUNKS, rows, layers * wide), jnp.bfloat16),
             pltpu.VMEM((devices, 1, devices * local), jnp.float32),
+            pltpu.VMEM((local, basis_out.shape[1] // 2, 2 * basis_out.shape[1]), jnp.float32),
             pltpu.SemaphoreType.DMA((CHUNKS, layers)),
             pltpu.SemaphoreType.DMA((CHUNKS, devices)),
             pltpu.SemaphoreType.DMA((CHUNKS, devices)),
@@ -210,7 +275,10 @@
             flops=2 * rows * layers * proj * devices * count,
             bytes_accessed=layers * rows * proj * 2, transcendentals=0,
         ),
-    )(mine, token_counts.reshape(rows, 1), train_grads)
+    )(
+        queries, token_counts.reshape(1, rows), basis_out, basis_in, eig_out, eig_in, train_grads
+    )
+    return flat.T
 
 
 def solution(mesh):
@@ -220,7 +288,7 @@
         layers, rows, proj = train_grads.shape
         local = layers * queries.shape[1]
         fits = devices % 4 == 0 and local % 16 == 0 and proj % (128 * CHUNKS) == 0
-        fits = fits and devices * local <= 512 and rows % 16 == 0
+        fits = fits and proj == 4096 and devices * local <= 512 and rows % 16 == 0
         fits = fits and layers * rows * proj <= 12 * 2**20
         body = fused if fits else plain
         return body(train_grads, token_counts, queries, *factors)

time: 56.7 us -> 45.5 us (0.80)
  matrix products: 4.35 us -> 0 us
  Pallas kernels: 45.6 us -> 42.5 us
  local copies, waits for them, and re-layouts: 5.61 us -> 2.86 us
  other arithmetic: 0.83 us -> 0 us
    dot_general x4 -> x0, matrix products: 4.35 us -> none  [the longest x1 1.9 us: precondition(): jnp.einsum('lji,lnjm->lnim', basis_out, rotated, precision=HIGHEST)]
    pallas_call x1, Pallas kernels: 45.6 us -> 42.5 us  [fused(): pl.pallas_call(functools.partial(kernel, devices, layers), out_shape=jax....]
    pallas_call x1 -> x0, local copies, waits for them, and re-layouts: 1.79 us -> none  [fused(): pl.pallas_call(functools.partial(kernel, devices, layers), out_shape=jax....]
    unnamed x2 -> x1, local copies, waits for them, and re-layouts: 0.01 us -> 1.59 us
    reshape x2 -> x1, local copies, waits for them, and re-layouts: 2.7 us -> 1.27 us  [fused(): token_counts.reshape(1, rows)]
    convert_element_type x2 -> x0, local copies, waits for them, and re-layouts: 1.11 us -> none  [precondition(): return back.reshape(layers, count, proj).astype(jnp.bfloat16)]
    add x1 -> x0, other arithmetic: 0.83 us -> none  [precondition(): spectrum = eig_out[:, :, None] * eig_in[:, None, :] + 0.01]
where the time goes in v2:
time: 45.5 us; the launch traced here: 45.4 us
  Pallas kernels  42.5 us (93%)
  local copies, waits for them, and re-layouts  2.86 us (6%)
    pallas_call x1, Pallas kernels, fused(): pl.pallas_call(functools.partial(kernel, devices, layers), out_shape=jax....  42.5 us
    unnamed x1, local copies, waits for them, and re-layouts  1.59 us
    reshape x1, local copies, waits for them, and re-layouts, fused(): token_counts.reshape(1, rows)  1.27 us

profile of v2, /device:TPU:0, one launch (start us, length us, event | category | flops | bytes accessed | tf_op | source)
XLA Modules:
  0.0 45.4 jit_solution(13660107323754600866)
XLA Ops:
  0.0 1.3 %reshape.3.counts_ref = s32[1,640]{1,0:T(1,128)} reshape(s32[640]{0:T(1024)} %param.8) | data formatting | bytes 5120 | tf_op jit(solution)/shard_map/reshape | solution.py:279
  1.3 42.5 %shard_map.73 = f32[64,640]{1,0:T(8,128)} custom-call(bf16[4,4,4096]{2,1,0:T(4,128)(2,1)} %raw_ref.1, s32[1,640]{1,0:T(1,128)} %reshape.3.counts_ref, f32[4,64,64]{2,1,0:T(8,128)} %basis_out_ref.1, f32[4,64,64]{2,1,0:T(8,128)} %basis_in_ref.1, f32[4,64]{1,0:T(4,128)} %eig_out_ref.1, f32[4,64]{1,0:T(4,128)} %eig_in_ref.1, bf16[4,640,4096]{2,1,0:T(8,128)(2,1)} %train_ref.1), custom_call_target="tpu_custom_call" | custom-call | flops 1342177280 | bytes 20971520 | tf_op jit(solution)/shard_map/pallas_call | solution.py:255
  43.8 1.6 %copy.9 = f32[640,64]{0,1:T(8,128)} copy(f32[640,64]{0,1:T(8,128)} %bitcast.1) | data formatting | bytes 327680

commit v3 on v2

--- a/solution.py
+++ b/solution.py
@@ -52,10 +52,15 @@
 
 
 def dot(a, b, over_a=1, over_b=0):
-    return lax.dot_general(
-        a, b, (((over_a,), (over_b,)), ((), ())),
-        precision=HIGHEST, preferred_element_type=jnp.float32,
-    )
+    def product(left, right):
+        return lax.dot_general(
+            left, right, (((over_a,), (over_b,)), ((), ())), preferred_element_type=jnp.float32
+        )
+
+    a_high, b_high = a.astype(jnp.bfloat16), b.astype(jnp.bfloat16)
+    a_low = (a - a_high.astype(jnp.float32)).astype(jnp.bfloat16)
+    b_low = (b - b_high.astype(jnp.float32)).astype(jnp.bfloat16)
+    return product(a_high, b_high) + (product(a_high, b_low) + product(a_low, b_high))
 
 
 def condition_into(
@@ -102,7 +107,7 @@
 
 def kernel(
     devices, layers, raw_ref, counts_ref, basis_out_ref, basis_in_ref, eig_out_ref, eig_in_ref,
-    train_ref, out_ref, held, rows_of, sums, field, load_sem, send_sem, recv_sem, sum_send, sum_recv,
+    train_ref, out_ref, mean_ref, held, rows_of, sums, field, load_sem, send_sem, recv_sem, sum_send, sum_recv,
 ):
     me = lax.axis_index("train")
     depth = devices // 4
@@ -137,7 +142,7 @@
     condition_into(
         held.at[me], field, raw_ref, basis_out_ref, basis_in_ref, eig_out_ref, eig_in_ref
     )
-    inverse = column_of(1.0 / counts_ref[...].astype(jnp.float32))
+    inverse = column_of(1.0 / counts_ref[...].reshape(1, counts_ref.shape[0]).astype(jnp.float32))
     pl.semaphore_wait(barrier, devices - 1)
 
     sent = []
@@ -227,6 +232,7 @@
         jnp.where(pick, 1.0, 0.0), scores, (((1,), (1,)), ((), ())),
         precision=HIGHEST, preferred_element_type=jnp.float32,
     )
+    out_ref[...] = flat
     for step in range(1, devices):
         which = (me + step) % devices
         pltpu.make_async_remote_copy(
@@ -240,7 +246,7 @@
     mean = summed * (1.0 / (devices * scores.shape[0]))
     mean = jnp.broadcast_to(mean, (queries, total_rows))
     mean = jnp.sum(jnp.where(pick, mean, 0.0), axis=1, keepdims=True)
-    out_ref[...] = flat - mean
+    mean_ref[...] = mean
     for copy in sent + told:
         copy.wait_send()
 
@@ -252,11 +258,14 @@
     local = layers * count
     wide = proj // CHUNKS
     vmem = pl.BlockSpec(memory_space=pltpu.VMEM)
-    flat = pl.pallas_call(
+    flat, mean = pl.pallas_call(
         functools.partial(kernel, devices, layers),
-        out_shape=jax.ShapeDtypeStruct((devices * count, rows), jnp.float32),
+        out_shape=[
+            jax.ShapeDtypeStruct((devices * count, rows), jnp.float32),
+            jax.ShapeDtypeStruct((devices * count, 1), jnp.float32),
+        ],
         in_specs=[vmem] * 6 + [pl.BlockSpec(memory_space=pl.ANY)],
-        out_specs=vmem,
+        out_specs=[vmem, vmem],
         scratch_shapes=[
             pltpu.VMEM((devices, local, proj), jnp.bfloat16),
             pltpu.VMEM((CHUNKS, rows, layers * wide), jnp.bfloat16),
@@ -276,9 +285,9 @@
             bytes_accessed=layers * rows * proj * 2, transcendentals=0,
         ),
     )(
-        queries, token_counts.reshape(1, rows), basis_out, basis_in, eig_out, eig_in, train_grads
+        queries, token_counts, basis_out, basis_in, eig_out, eig_in, train_grads
     )
-    return flat.T
+    return (flat - mean).T
 
 
 def solution(mesh):

time: 45.5 us -> 42.9 us (0.943)
  local copies, waits for them, and re-layouts: 2.86 us -> 0 us
  other arithmetic: 0 us -> 2.54 us
  Pallas kernels: 42.5 us -> 40.1 us
    pallas_call x1, Pallas kernels: 42.5 us -> 40.1 us  [fused(): pl.pallas_call(functools.partial(kernel, devices, layers), out_shape=[jax...]
    transpose x0 -> x1, other arithmetic: none -> 1.67 us  [fused(): return (flat - mean).T]
    unnamed x1 -> x0, local copies, waits for them, and re-layouts: 1.59 us -> none
    reshape x1 -> x0, local copies, waits for them, and re-layouts: 1.27 us -> none  [fused(): token_counts.reshape(1, rows)]
    pallas_call x0 -> x1, other arithmetic: none -> 0.87 us  [fused(): pl.pallas_call(functools.partial(kernel, devices, layers), out_shape=[jax...]
where the time goes in v3:
time: 42.9 us; the launch traced here: 42.6 us
  Pallas kernels  40.1 us (93%)
  other arithmetic  2.54 us (6%)
    pallas_call x1, Pallas kernels, fused(): pl.pallas_call(functools.partial(kernel, devices, layers), out_shape=[jax...  40.1 us
    transpose x1, other arithmetic, fused(): return (flat - mean).T  1.67 us
    pallas_call x1, other arithmetic, fused(): pl.pallas_call(functools.partial(kernel, devices, layers), out_shape=[jax...  0.87 us

profile of v3, /device:TPU:0, one launch (start us, length us, event | category | flops | bytes accessed | tf_op | source)
XLA Modules:
  0.0 42.6 jit_solution(18380228179427373724)
XLA Ops:
  0.0 40.1 %shard_map.73 = (f32[64,640]{1,0:T(8,128)}, f32[64,1]{1,0:T(8,128)}) custom-call(bf16[4,4,4096]{2,1,0:T(4,128)(2,1)} %raw_ref.1, s32[640]{0:T(1024)} %counts_ref.1, f32[4,64,64]{2,1,0:T(8,128)} %basis_out_ref.1, f32[4,64,64]{2,1,0:T(8,128)} %basis_in_ref.1, f32[4,64]{1,0:T(4,128)} %eig_out_ref.1, f32[4,64]{1,0:T(4,128)} %eig_in_ref.1, ...), custom_call_target="tpu_custom_call" | custom-call | flops 1342177280 | bytes 20971520 | tf_op jit(solution)/shard_map/pallas_call | solution.py:261
  40.1 0.9 %reduce = f32[64]{0:T(128)S(1)} reduce(f32[64,1]{1,0:T(8,128)} %get-tuple-element.8, f32[]{:T(128)} %constant.1), dimensions={1}, to_apply=%get-tuple-element.8.reduce_sub_computation | reduce | bytes 516 | tf_op jit(solution)/shard_map/pallas_call | solution.py:261
  41.0 1.7 %subtract_bitcast_fusion = f32[640,64]{0,1:T(8,128)} fusion(f32[64,640]{1,0:T(8,128)} %get-tuple-element.7, f32[64]{0:T(128)S(1)} %reduce), kind=kLoop, calls=%fused_computation | loop fusion | flops 40960 | bytes 327936 | tf_op jit(solution)/shard_map/transpose | solution.py:290
